TPU v7x, 128 devices: a whole 4x4x4 slice. The times are simulated.
128 devices in a mesh: cell: 16 (over y, x), station: 8 (over z, core).
Axes of the slice: x: 4, y: 4, z: 4, core: 2. Of those that a mesh axis runs over, the one named last changes fastest.
Arguments:
- sensitivity: float32 [2048, 262144], P('station', 'cell'), may hold values from -6 to 6
- tile_mask: int32 [16, 512], P('station', 'cell'), may hold values 0 or 1
- data_panel: float32 [32, 2048], P('cell', 'station'), may hold values from -6 to 6
- model_panel: float32 [32, 262144], P('station', 'cell'), may hold values from -6 to 6
Outputs:
- data_vector: float32 [2048], P('station')
- model_vector: float32 [262144], P('cell')
- bidiag: float32 [4], replicated
All inputs are finite; a program needn't handle non-finite values. No bound on the sum of `tile_mask` on one device may be relied on, other than what follows from the above.
Results may differ from a plain program's by a relative error of at most 0.0003.
Values sent between devices are 32-bit elements; how exact they have to be, the bound alone decides.
A program may use at most 128 MiB of HBM per device.

v0:
```python
import math

import jax
import jax.numpy as jnp
from jax import lax
from jax.sharding import PartitionSpec as P

TILE_ROWS = 128
TILE_COLS = 512


HIGH = lax.Precision.HIGHEST


def orthonormal(panel, gram):
    lower = jnp.linalg.cholesky(gram)
    return lax.linalg.triangular_solve(lower, panel, left_side=True, lower=True)


def project(vector, basis, reducer):
    local_coef = jnp.dot(basis, vector, precision=HIGH)
    coef = reducer(local_coef)
    rest = vector - jnp.dot(coef, basis, precision=HIGH)
    norm = jnp.sqrt(reducer(jnp.sum(rest * rest)))
    return (rest / norm, norm)


def model_reduce(value):
    return lax.psum(value, "cell")


def data_reduce(value):
    return lax.psum(value, "station")


def model_whole_basis(model_panel):
    model_full = lax.all_gather(model_panel, "station", axis=0, tiled=True)
    gram_model = lax.psum(jnp.dot(model_full, model_full.T, precision=HIGH), "cell")
    return orthonormal(model_full, gram_model)


def per_device(sensitivity, tile_mask, data_panel, model_panel):
    rows, cols = sensitivity.shape
    weights = tile_mask.astype(jnp.float32)
    masked = (
        sensitivity.reshape(rows // TILE_ROWS, TILE_ROWS, cols // TILE_COLS, TILE_COLS)
        * weights[:, None, :, None]
    ).reshape(rows, cols)
    total_rows = rows * lax.axis_size("station")
    total_cols = cols * lax.axis_size("cell")
    data_full = lax.all_gather(data_panel, "cell", axis=0, tiled=True)
    gram_data = lax.psum(jnp.dot(data_full, data_full.T, precision=HIGH), "station")
    basis_u = orthonormal(data_full, gram_data)
    start = basis_u[-1]
    basis_v = model_whole_basis(model_panel)

    def adjoint_whole(vector):
        return lax.psum(jnp.dot(vector, masked, precision=HIGH), "station")

    def forward_whole(vector):
        return lax.psum(jnp.dot(masked, vector, precision=HIGH), "cell")

    first_v, alpha_one = project(adjoint_whole(start), basis_v, model_reduce)
    first_u, beta_one = project(forward_whole(first_v), basis_u, data_reduce)
    second_v, alpha_two = project(
        adjoint_whole(first_u), jnp.concatenate([basis_v, first_v[None, :]], axis=0), model_reduce
    )
    second_u, beta_two = project(
        forward_whole(second_v), jnp.concatenate([basis_u, first_u[None, :]], axis=0), data_reduce
    )
    bidiag = jnp.stack(
        [
            alpha_one / math.sqrt(total_cols),
            beta_one / math.sqrt(total_rows),
            alpha_two / math.sqrt(total_cols),
            beta_two / math.sqrt(total_rows),
        ]
    )
    return (second_u * math.sqrt(total_rows), second_v * math.sqrt(total_cols), bidiag)


def solution(mesh):
    placed = (
        P("station", "cell"),
        P("station", "cell"),
        P("cell", "station"),
        P("station", "cell"),
    )
    return jax.shard_map(
        per_device,
        mesh=mesh,
        in_specs=placed,
        out_specs=(P("station"), P("cell"), P()),
        check_vma=False,
    )
```

profile of v0, /device:TPU:1, one launch (start us, length us, event | category | flops | bytes accessed | tf_op | source)
XLA Modules:
  0.0 583.1 jit_solution(14035551248422658549)
XLA Ops:
  7.2 0.7 all-gather.4.cloned.1.call-update
  7.9 0.7 convert_element_type.3
  8.6 2.2 mul.35
  10.8 13.8 %copy.17 = f32[32,8,32,512]{3,1,2,0:T(8,128)} copy(f32[32,8,32,512]{3,2,1,0:T(8,128)S(1)} %bitcast.90) | data formatting | bytes 33554432
  24.6 20.0 %all-gather = f32[16,2,256]{2,1,0:T(2,128)S(1)} all-gather(f32[1,2,256]{2,1,0:T(2,128)S(1)} %bitcast.111), channel_id=1, replica_groups=mesh['cell'=16,'station'=8] {'cell'}, dimensions={0}, use_global_device_ids=true | all-gather | bytes 34816 | tf_op jit(solution)/shard_map/all_gather | solution.py:51
  44.6 0.2 fusion.23
  44.8 26.8 %psum.98 = f32[32,32]{0,1:T(8,128)S(1)} all-reduce(f32[32,32]{0,1:T(8,128)S(1)} %fusion.23), channel_id=1, replica_groups=mesh['cell'=16,'station'=8] {'station'}, use_global_device_ids=true, to_apply=%region_0.0 | all-reduce | flops 1024 | bytes 8192 | tf_op jit(solution)/shard_map/psum | solution.py:52
  71.7 2.9 cholesky.44
  74.6 0.6 compare_reduce_fusion.1
  75.3 0.7 fusion.4
  75.9 2.4 custom-call.8
  78.4 11.3 %mul.37 = f32[256,16384]{1,0:T(8,128)S(1)} multiply(f32[256,16384]{1,0:T(8,128)} %param.5, f32[256,16384]{1,0:T(8,128)} %bitcast.89) | non-fusion elementwise | flops 4194304 | bytes 50331648 | tf_op jit(solution)/shard_map/mul | solution.py:46
  89.7 0.2 fusion.9
  89.9 8.6 %fusion.12 = f32[1,16384]{1,0:T(1,128)} fusion(f32[256,16384]{1,0:T(8,128)S(1)} %mul.37, f32[32,256]{1,0:T(8,128)S(1)} %fusion.9), kind=kOutput, calls=%fused_computation.33 | convolution fusion | flops 50331648 | bytes 16843776 | tf_op jit(solution)/shard_map/dot_general | solution.py:58
  98.6 2.0 reshape.24
  100.6 1.8 fusion.24
  102.4 58.5 %psum.100 = f32[32,32]{0,1:T(8,128)S(1)} all-reduce(f32[32,32]{0,1:T(8,128)S(1)} %fusion.24), channel_id=1, replica_groups=mesh['cell'=16,'station'=8] {'cell'}, use_global_device_ids=true, to_apply=%region_4.0 | all-reduce | flops 1024 | bytes 8192 | tf_op jit(solution)/shard_map/psum | solution.py:38
  160.9 2.9 cholesky.55
  163.9 0.6 compare_reduce_fusion
  164.5 0.7 fusion.5
  165.2 2.4 custom-call.9
  167.6 3.5 fusion.6
  171.2 2.6 convolution_bitcast_fusion.2
  173.8 28.5 %psum.101 = f32[32]{0:T(128)S(1)} all-reduce(f32[32]{0:T(128)S(1)} %convolution_bitcast_fusion.2), channel_id=1, replica_groups=mesh['cell'=16,'station'=8] {'cell'}, use_global_device_ids=true, to_apply=%region_5.0 | all-reduce | flops 32 | bytes 256 | tf_op jit(solution)/shard_map/psum | solution.py:29
  202.3 1.1 fusion.17
  203.4 0.6 multiply_reduce_fusion.1
  204.0 30.9 %psum.102 = f32[]{:T(128)} all-reduce(f32[]{:T(128)} %get-tuple-element.12), channel_id=1, replica_groups=mesh['cell'=16,'station'=8] {'cell'}, use_global_device_ids=true, to_apply=%region_7.0 | all-reduce | flops 1 | bytes 8 | tf_op jit(solution)/shard_map/psum | solution.py:29
  235.6 16.1 %fusion.25 = f32[1,256]{1,0:T(1,128)S(1)} fusion(f32[256,16384]{1,0:T(8,128)} %copy-done, f32[16384,1]{0,1:T(1,128)S(1)} %bitcast.91), kind=kOutput, calls=%fused_computation.51 | convolution fusion | flops 50331648 | bytes 16843776 | tf_op jit(solution)/shard_map/dot_general | solution.py:61
  251.7 28.5 %psum.103 = f32[256]{0:T(256)S(1)} all-reduce(f32[256]{0:T(256)S(1)} %bitcast.108), channel_id=1, replica_groups=mesh['cell'=16,'station'=8] {'cell'}, use_global_device_ids=true, to_apply=%region_8.0 | all-reduce | flops 256 | bytes 2048 | tf_op jit(solution)/shard_map/psum | solution.py:61
  280.3 50.3 %psum.104 = f32[32]{0:T(128)S(1)} all-reduce(f32[32]{0:T(128)S(1)} %convolution_bitcast_fusion.1), channel_id=1, replica_groups=mesh['cell'=16,'station'=8] {'station'}, use_global_device_ids=true, to_apply=%region_9.0 | all-reduce | flops 32 | bytes 256 | tf_op jit(solution)/shard_map/psum | solution.py:33
  330.7 0.6 multiply_reduce_fusion.3
  331.4 13.2 %psum.105 = f32[]{:T(128)} all-reduce(f32[]{:T(128)} %get-tuple-element.10), channel_id=1, replica_groups=mesh['cell'=16,'station'=8] {'station'}, use_global_device_ids=true, to_apply=%region_11.0 | all-reduce | flops 1 | bytes 8 | tf_op jit(solution)/shard_map/psum | solution.py:33
  345.3 12.1 %fusion.26 = f32[1,16384]{1,0:T(1,128)} fusion(f32[256,1]{0,1:T(1,128)S(1)} %bitcast.102, f32[256,16384]{1,0:T(8,128)} %copy-done), kind=kOutput, calls=%fused_computation.52 | convolution fusion | flops 50331648 | bytes 16843776 | tf_op jit(solution)/shard_map/dot_general | solution.py:58
  357.4 52.2 %all-reduce.5.cloned.1.call-done = f32[16384]{0:T(1024)} async-done(((f32[16384]{0:T(1024)}), f32[16384]{0:T(1024)}) %all-reduce.5.cloned.1.call-update) | async-done | bytes 65552 | tf_op jit(solution)/shard_map/psum | solution.py:58
  409.6 3.0 fusion.2
  412.7 33.3 %psum.107 = f32[33]{0:T(128)S(1)} all-reduce(f32[33]{0:T(128)S(1)} %fusion.2), channel_id=1, replica_groups=mesh['cell'=16,'station'=8] {'cell'}, use_global_device_ids=true, to_apply=%region_13.0 | all-reduce | flops 33 | bytes 264 | tf_op jit(solution)/shard_map/psum | solution.py:29
  446.0 1.4 fusion
  447.4 0.6 multiply_reduce_fusion
  448.0 29.2 %psum.108 = f32[]{:T(128)} all-reduce(f32[]{:T(128)} %get-tuple-element.8), channel_id=1, replica_groups=mesh['cell'=16,'station'=8] {'cell'}, use_global_device_ids=true, to_apply=%region_15.0 | all-reduce | flops 1 | bytes 8 | tf_op jit(solution)/shard_map/psum | solution.py:29
  478.0 0.6 broadcast_multiply_fusion
  478.6 16.1 %fusion.27 = f32[1,256]{1,0:T(1,128)S(1)} fusion(f32[256,16384]{1,0:T(8,128)} %copy-done, f32[16384,1]{0,1:T(1,128)S(1)} %bitcast.94), kind=kOutput, calls=%fused_computation.53 | convolution fusion | flops 50331648 | bytes 16843776 | tf_op jit(solution)/shard_map/dot_general | solution.py:61
  494.7 30.2 %psum.109 = f32[256]{0:T(256)S(1)} all-reduce(f32[256]{0:T(256)S(1)} %bitcast.107), channel_id=1, replica_groups=mesh['cell'=16,'station'=8] {'cell'}, use_global_device_ids=true, to_apply=%region_16.0 | all-reduce | flops 256 | bytes 2048 | tf_op jit(solution)/shard_map/psum | solution.py:61
  524.9 0.1 convolution_bitcast_fusion
  525.0 35.7 %psum.110 = f32[33]{0:T(128)S(1)} all-reduce(f32[33]{0:T(128)S(1)} %convolution_bitcast_fusion), channel_id=1, replica_groups=mesh['cell'=16,'station'=8] {'station'}, use_global_device_ids=true, to_apply=%region_17.0 | all-reduce | flops 33 | bytes 264 | tf_op jit(solution)/shard_map/psum | solution.py:33
  560.8 0.6 multiply_reduce_fusion.2
  561.4 13.0 %psum.111 = f32[]{:T(128)} all-reduce(f32[]{:T(128)} %get-tuple-element.6), channel_id=1, replica_groups=mesh['cell'=16,'station'=8] {'station'}, use_global_device_ids=true, to_apply=%region_19.21 | all-reduce | flops 1 | bytes 8 | tf_op jit(solution)/shard_map/psum | solution.py:33
  575.1 0.6 divide_multiply_fusion
  575.7 0.6 pad_maximum_fusion.8
  (29 shorter events, 0.9 us)
Async XLA Ops:
  7.2 91.4 %all-gather.4.cloned.1.call-start = ((), (), s32[]{:S(2)}) async-start(), calls=%async_computation.2 | async-start | bytes 2359296 | tf_op jit(solution)/shard_map/all_gather | solution.py:37
  7.9 163.2 %all-reduce.3.cloned.1.call-start = ((), (), s32[]{:S(2)}) async-start(), calls=%async_computation | async-start | bytes 131072 | tf_op jit(solution)/shard_map/psum | solution.py:58
  10.8 13.8 %copy-start.4 = (f32[2,256]{1,0:T(2,128)S(1)}, f32[2,256]{1,0:T(2,128)}, u32[]{:S(2)}) copy-start(f32[2,256]{1,0:T(2,128)} %param.7) | copy-start | bytes 6148
  89.7 8.8 %copy-start = (f32[256,16384]{1,0:T(8,128)}, f32[256,16384]{1,0:T(8,128)S(1)}, u32[]{:S(2)}) copy-start(f32[256,16384]{1,0:T(8,128)S(1)} %mul.37) | copy-start | bytes 50331652
  98.5 311.1 %all-reduce.5.cloned.1.call-start = ((), (), s32[]{:S(2)}) async-start(), calls=%async_computation.1 | async-start | bytes 131072 | tf_op jit(solution)/shard_map/psum | solution.py:58
  100.6 64.6 %copy-start.1 = (f32[32,16384]{1,0:T(8,128)}, f32[32,16384]{1,0:T(8,128)S(1)}, u32[]{:S(2)}) copy-start(f32[32,16384]{1,0:T(8,128)S(1)} %reshape.24) | copy-start | bytes 6291460
  171.1 32.2 %copy-start.2 = (f32[16384]{0:T(1024)S(1)}, f32[16384]{0:T(1024)}, u32[]{:S(2)}) copy-start(f32[16384]{0:T(1024)} %all-reduce.3.cloned.1.call-done) | copy-start | bytes 196612
  409.6 37.8 %copy-start.3 = (f32[16384]{0:T(1024)S(1)}, f32[16384]{0:T(1024)}, u32[]{:S(2)}) copy-start(f32[16384]{0:T(1024)} %all-reduce.5.cloned.1.call-done) | copy-start | bytes 196612
Sparse Core Ops, SparseCore 0:
  9.7 28.9 all-gather.3
  98.7 56.5 all-reduce.2
  357.5 52.0 all-reduce.4
where the time goes:
time: 588 us; the launch traced here: 583 us
  blocking collectives  398 us (68%)
  matrix products  67.1 us (11%)
  waiting for transfers between devices  53 us (9%)
  other arithmetic  29.7 us (5%)
  local copies, waits for them, and re-layouts  18.1 us (3%)
  between operations  16.9 us (3%)
    psum x4, blocking collectives, model_reduce(): return lax.psum(value, 'cell')  122 us
    psum x4, blocking collectives, data_reduce(): return lax.psum(value, 'station')  112 us
    psum x2, blocking collectives, forward_whole(): return lax.psum(jnp.dot(masked, vector, precision=HIGH), 'cell')  58.7 us
    psum x1, blocking collectives, model_whole_basis(): lax.psum(jnp.dot(model_full, model_full.T, precision=HIGH), 'cell')  58.5 us
    psum x2, waiting for transfers between devices, adjoint_whole(): return lax.psum(jnp.dot(vector, masked, precision=HIGH), 'station')  52.2 us
    dot_general x2, matrix products, forward_whole(): return lax.psum(jnp.dot(masked, vector, precision=HIGH), 'cell')  32.1 us
    psum x1, blocking collectives, per_device(): lax.psum(jnp.dot(data_full, data_full.T, precision=HIGH), 'station')  26.8 us
    dot_general x2, matrix products, adjoint_whole(): return lax.psum(jnp.dot(vector, masked, precision=HIGH), 'station')  20.6 us
  transfers between devices with their start and end apart: 3, of which 1 were waited for; matrix products, arithmetic and copies ran while one was open for 10% of the time, Pallas kernels for 0%

commit v1 on v0

v1 whole, which is shorter than its diff:
```python
import functools
import math

import jax
import jax.numpy as jnp
from jax import lax
from jax.experimental import pallas as pl
from jax.experimental.pallas import tpu as pltpu
from jax.sharding import PartitionSpec as P

TILE_ROWS = 128
TILE_COLS = 512
LANES = 128
HIGH = lax.Precision.HIGHEST
MESH = pl.DeviceIdType.MESH
F32 = jnp.float32


def eye_mask(rows):
    return lax.broadcasted_iota(jnp.int32, (rows, LANES), 0) == lax.broadcasted_iota(jnp.int32, (rows, LANES), 1)


def to_lanes(column, rows):
    return jnp.sum(jnp.where(eye_mask(rows), column, 0.0), axis=0, keepdims=True)


def to_rows(row, rows):
    return jnp.sum(jnp.where(eye_mask(rows), row, 0.0), axis=1, keepdims=True)


def lane(row, index):
    ids = lax.broadcasted_iota(jnp.int32, (1, LANES), 1)
    return jnp.sum(jnp.where(ids == index, row, 0.0), axis=1, keepdims=True)


def put_lane(row, index, value):
    ids = lax.broadcasted_iota(jnp.int32, (1, LANES), 1)
    return jnp.where(ids == index, value, row)


def total(x):
    return jnp.sum(jnp.sum(x, axis=0, keepdims=True), axis=1, keepdims=True)


def dot_t(a, b):
    return lax.dot_general(a, b, (((1,), (1,)), ((), ())), precision=HIGH, preferred_element_type=F32)


def pack(gram):
    rows = gram.shape[0] // 4
    return jnp.concatenate([gram[q * rows : (q + 1) * rows, :] for q in range(4)], axis=1)


def unpack(packed, size):
    return jnp.concatenate([packed[:, q * size : (q + 1) * size] for q in range(4)], axis=0)


def inverse(gram, size):
    rows = lax.broadcasted_iota(jnp.int32, (size, LANES), 0)
    unit = jnp.where(
        rows + size == lax.broadcasted_iota(jnp.int32, (size, LANES), 1), 1.0, 0.0
    )
    a = jnp.concatenate([gram, jnp.zeros((size, LANES - size), F32)], axis=1) + unit
    for i in range(size):
        pivot_row = a[i : i + 1, :] / a[i : i + 1, i : i + 1]
        a = jnp.where(rows == i, pivot_row, a - a[:, i : i + 1] * pivot_row)
    return jnp.concatenate([a[:, size : 2 * size], jnp.zeros((size, LANES - size), F32)], axis=1)


def kernel(
    nc, ns, total_rows, total_cols,
    sens, mask, dp, mp,
    out_u, out_v, out_b,
    g, pfull, pown, plocal, d1, p64, gu, gmc, gms,
    wpart, rs, ag, cc, cs, rbuf, fx, us, last, ub, stack, ybuf,
    load_sem, send, recv, zrecv, relay_sem, bulk_send,
):
    me_c, me_s = lax.axis_index("cell"), lax.axis_index("station")
    nz = ns // 2
    z, core = me_s // 2, me_s % 2
    partner = z * 2 + (1 - core)
    rows, cols = sens.shape
    tiles = cols // LANES
    own = tiles // ns
    kd, km = dp.shape[0], mp.shape[0]
    size = kd * nc
    halves = rows // LANES
    per = TILE_COLS // LANES

    load_rows = rows // 8
    loads = [
        pltpu.make_async_copy(
            sens.at[pl.ds(q * load_rows, load_rows), :], g.at[pl.ds(q * load_rows, load_rows), :], load_sem.at[q]
        )
        for q in range(8)
    ]
    load_panel = pltpu.make_async_copy(mp, plocal, load_sem.at[8])
    load_panel.start()
    for copy in loads:
        copy.start()

    barrier = pltpu.get_barrier_semaphore()
    for d in range(1, nc):
        pl.semaphore_signal(barrier, inc=1, device_id={"cell": (me_c + d) % nc}, device_id_type=MESH)
    for d in range(1, ns):
        pl.semaphore_signal(barrier, inc=1, device_id={"station": (me_s + d) % ns}, device_id_type=MESH)

    drains = []

    def exchange(axis, src, dst, index):
        n, me = (nc, me_c) if axis == "cell" else (ns, me_s)
        for d in range(1, n):
            peer = (me + d) % n
            pltpu.make_async_remote_copy(
                src_ref=src(peer), dst_ref=dst, send_sem=send.at[index], recv_sem=recv.at[index],
                device_id={axis: peer}, device_id_type=MESH,
            ).start()

    def settle(index, span):
        pltpu.make_async_copy(span, span, recv.at[index]).wait()
        drains.append((index, span))

    block = dp[...]
    for h in range(halves):
        d1[me_c, h * kd : (h + 1) * kd, :] = block[:, h * LANES : (h + 1) * LANES]

    load_panel.wait()

    @pl.loop(0, tiles)
    def _(j):
        piece = plocal[:, pl.ds(pl.multiple_of(j * LANES, LANES), LANES)]
        for k in range(km):
            pfull[me_s * km + k, pl.ds(j, 1), :] = piece[k : k + 1, :]

    pl.semaphore_wait(barrier, nc + ns - 2)

    exchange("cell", lambda peer: d1.at[me_c], d1.at[me_c], 0)
    mine = pl.ds(me_s * km, km)
    exchange(
        "station",
        lambda peer: pfull.at[mine, pl.ds(pl.multiple_of(peer * own, own), own), :],
        pown.at[mine, :, :],
        1,
    )
    bulk = []
    for d in range(1, nz):
        copy = pltpu.make_async_remote_copy(
            src_ref=pfull.at[mine], dst_ref=pfull.at[mine], send_sem=bulk_send.at[d], recv_sem=zrecv.at[d],
            device_id={"station": ((z + d) % nz) * 2 + core}, device_id_type=MESH,
        )
        copy.start()
        bulk.append(copy)
    copy = pltpu.make_async_remote_copy(
        src_ref=pfull.at[mine], dst_ref=pfull.at[mine], send_sem=bulk_send.at[0], recv_sem=zrecv.at[0],
        device_id={"station": partner}, device_id_type=MESH,
    )
    copy.start()
    bulk.insert(0, copy)
    pown[mine, :, :] = pfull[mine, pl.ds(pl.multiple_of(me_s * own, own), own), :]

    settle(0, d1.at[pl.ds(0, nc - 1)])
    for c in range(nc):
        for h in range(halves):
            p64[h, c * kd : (c + 1) * kd, :] = d1[c, h * kd : (h + 1) * kd, :]
    gram = dot_t(p64[0], p64[0])
    for h in range(1, halves):
        gram = gram + dot_t(p64[h], p64[h])
    gu[me_s] = pack(gram)
    exchange("station", lambda peer: gu.at[me_s], gu.at[me_s], 2)

    settle(1, pown.at[pl.ds(0, km * (ns - 1))])
    mine_all = jnp.concatenate([pown[:, j, :] for j in range(own)], axis=1)
    gmc[me_c] = pack(dot_t(mine_all, mine_all))
    exchange("cell", lambda peer: gmc.at[me_c], gmc.at[me_c], 3)

    settle(2, gu.at[pl.ds(0, ns - 1)])
    t_u = inverse(unpack(jnp.sum(gu[...], axis=0), size), size)
    x_col = t_u[:, size - 1 : size] / jnp.sqrt(t_u[size - 1 : size, size - 1 : size])
    start = [jnp.sum(x_col * p64[h], axis=0, keepdims=True) for h in range(halves)]

    settle(3, gmc.at[pl.ds(0, nc - 1)])
    gms[me_s] = jnp.sum(gmc[...], axis=0)
    exchange("station", lambda peer: gms.at[me_s], gms.at[me_s], 4)

    for copy in loads:
        copy.wait()

    def adjoint(vector, t):
        for h in range(halves):
            ub[h * LANES : (h + 1) * LANES, :] = jnp.broadcast_to(to_rows(vector[h], LANES), (LANES, LANES))

        @pl.loop(0, tiles // per)
        def _(j):
            for q in range(per):
                at = pl.ds(pl.multiple_of((j * per + q) * LANES, LANES), LANES)
                result = None
                for h in range(halves):
                    parts = [None, None]
                    for r in range(h * LANES, (h + 1) * LANES, 8):
                        term = g[r : r + 8, at] * ub[r : r + 8, :]
                        w = (r // 8) % 2
                        parts[w] = term if parts[w] is None else parts[w] + term
                    part = (parts[0] + parts[1]) * mask[h, j].astype(F32)
                    result = part if result is None else result + part
                wpart[t, pl.ds(j * per + q, 1), :] = jnp.sum(result, axis=0, keepdims=True)

    def forward(t):
        def step(j, sums):
            sums = list(sums)
            for q in range(per):
                at = pl.ds(pl.multiple_of((j * per + q) * LANES, LANES), LANES)
                row = rbuf[t, pl.ds(j * per + q, 1), :]
                for h in range(halves):
                    sums[h] = sums[h] + g[h * LANES : (h + 1) * LANES, at] * (row * mask[h, j].astype(F32))
            return tuple(sums)

        sums = lax.fori_loop(0, tiles // per, step, tuple(jnp.zeros((LANES, LANES), F32) for _ in range(halves)))
        return [to_lanes(jnp.sum(part, axis=1, keepdims=True), LANES) for part in sums]

    def scatter(t, index):
        own_at = pl.ds(pl.multiple_of(me_s * own, own), own)
        rs[t, me_s] = wpart[t, own_at, :]
        exchange(
            "station",
            lambda peer: wpart.at[t, pl.ds(pl.multiple_of(peer * own, own), own), :],
            rs.at[t, me_s],
            index,
        )

    def gather(t, index_rs, index_ag):
        settle(index_rs, rs.at[t, pl.ds(0, ns - 1)])
        own_at = pl.ds(pl.multiple_of(me_s * own, own), own)
        w_own = jnp.sum(rs[t], axis=0)
        ag[t, own_at, :] = w_own
        exchange("station", lambda peer: ag.at[t, own_at, :], ag.at[t, own_at, :], index_ag)
        return w_own

    def reorthogonalise(t, w, coef, extra):
        y = jnp.sum(t_m * coef, axis=1, keepdims=True)
        ybuf[...] = jnp.broadcast_to(y, (size, LANES))
        rest = w if extra is None else w - extra

        def step(k, rest):
            return rest - pfull[k] * ybuf[pl.ds(k, 1), :]

        rest = lax.fori_loop(0, size, step, rest)
        rbuf[t] = rest
        return total(rest * rest)

    def data_side(t, index_fx, index_us, squares, before):
        parts = forward(t)
        for h in range(halves):
            fx[t, me_c, h : h + 1, :] = parts[h]
        fx[t, me_c, halves : halves + 1, :] = jnp.broadcast_to(squares, (1, LANES))
        fx[t, me_c, halves + 1 : halves + 2, :] = jnp.zeros((1, LANES), F32)
        exchange("cell", lambda peer: fx.at[t, me_c], fx.at[t, me_c], index_fx)
        settle(index_fx, fx.at[t, pl.ds(0, nc - 1)])
        summed = jnp.sum(fx[t], axis=0)
        norm = jnp.sqrt(summed[halves : halves + 1, 0:1])
        scale = 1.0 / norm
        vec = [summed[h : h + 1, :] * scale for h in range(halves)]
        col = p64[0] * vec[0]
        for h in range(1, halves):
            col = col + p64[h] * vec[h]
        coef = to_lanes(jnp.sum(col, axis=1, keepdims=True), size)
        if before is not None:
            along = sum(jnp.sum(before[h] * vec[h], axis=1, keepdims=True) for h in range(halves))
            coef = put_lane(coef, size, along)
        us[t, me_s] = coef
        exchange("station", lambda peer: us.at[t, me_s], us.at[t, me_s], index_us)
        settle(index_us, us.at[t, pl.ds(0, ns - 1)])
        coef = jnp.sum(us[t], axis=0)
        y = jnp.sum(t_u * coef, axis=1, keepdims=True)
        rest = [vec[h] - jnp.sum(y * p64[h], axis=0, keepdims=True) for h in range(halves)]
        if before is not None:
            along = lane(coef, size)
            rest = [rest[h] - along * before[h] for h in range(halves)]
        return rest, norm, scale

    def sum_squares(vector):
        return sum(jnp.sum(part * part, axis=1, keepdims=True) for part in vector)

    adjoint(start, 0)
    scatter(0, 5)
    w_own = gather(0, 5, 6)
    for k in range(size):
        stack[k : k + 1, :] = jnp.sum(pown[k] * w_own, axis=0, keepdims=True)
    cc[0, me_c] = to_lanes(jnp.sum(stack[0:size, :], axis=1, keepdims=True), size)
    exchange("cell", lambda peer: cc.at[0, me_c], cc.at[0, me_c], 7)
    settle(4, gms.at[pl.ds(0, ns - 1)])
    t_m = inverse(unpack(jnp.sum(gms[...], axis=0), size), size)
    for d in range(1, nz):
        bulk[d].wait_recv()
        theirs = pl.ds((((z + nz - d) % nz) * 2 + core) * km, km)
        copy = pltpu.make_async_remote_copy(
            src_ref=pfull.at[theirs], dst_ref=pfull.at[theirs], send_sem=relay_sem.at[0], recv_sem=relay_sem.at[1],
            device_id={"station": partner}, device_id_type=MESH,
        )
        copy.start()
    settle(7, cc.at[0, pl.ds(0, nc - 1)])
    cs[0, me_s] = jnp.sum(cc[0], axis=0)
    exchange("station", lambda peer: cs.at[0, me_s], cs.at[0, me_s], 8)
    bulk[0].wait_recv()
    relayed = pfull.at[pl.ds(0, km * (nz - 1))]
    pltpu.make_async_copy(relayed, relayed, relay_sem.at[1]).wait()
    settle(6, ag.at[0, pl.ds(0, own * (ns - 1)), :])
    settle(8, cs.at[0, pl.ds(0, ns - 1)])
    squares = reorthogonalise(0, ag[0], jnp.sum(cs[0], axis=0), None)
    rest_u, norm_v1, scale_v1 = data_side(0, 9, 10, squares, None)

    adjoint(rest_u, 1)
    scatter(1, 11)
    part = wpart[1]

    def step(k, carry):
        stack[pl.ds(k, 1), :] = jnp.sum(pfull[k] * part, axis=0, keepdims=True)
        return carry

    lax.fori_loop(0, size, step, 0)
    coef = to_lanes(jnp.sum(stack[0:size, :], axis=1, keepdims=True), size)
    coef = put_lane(coef, size, total(rbuf[0] * part) * scale_v1)
    cc[1, me_c] = coef
    exchange("cell", lambda peer: cc.at[1, me_c], cc.at[1, me_c], 12)
    gather(1, 11, 13)
    settle(12, cc.at[1, pl.ds(0, nc - 1)])
    cs[1, me_s] = put_lane(jnp.sum(cc[1], axis=0), size + 1, sum_squares(rest_u))
    exchange("station", lambda peer: cs.at[1, me_s], cs.at[1, me_s], 14)
    settle(13, ag.at[1, pl.ds(0, own * (ns - 1)), :])
    settle(14, cs.at[1, pl.ds(0, ns - 1)])
    coef = jnp.sum(cs[1], axis=0)
    norm_u1 = jnp.sqrt(lane(coef, size + 1))
    scale_u1 = 1.0 / norm_u1
    coef = coef * scale_u1
    along = rbuf[0] * (lane(coef, size) * scale_v1)
    squares = reorthogonalise(1, ag[1] * scale_u1, coef, along)
    first_u = [rest_u[h] * scale_u1 for h in range(halves)]
    rest_u, norm_v2, scale_v2 = data_side(1, 15, 16, squares, first_u)

    last[me_s] = jnp.broadcast_to(sum_squares(rest_u), (1, LANES))
    exchange("station", lambda peer: last.at[me_s], last.at[me_s], 17)
    out_v[...] = rbuf[1] * (scale_v2 * math.sqrt(total_cols))
    settle(17, last.at[pl.ds(0, ns - 1)])
    norm_u2 = jnp.sqrt(jnp.sum(last[...], axis=0)[:, 0:1])
    for h in range(halves):
        out_u[h : h + 1, :] = rest_u[h] * (math.sqrt(total_rows) / norm_u2)
    row = jnp.zeros((1, LANES), F32)
    row = put_lane(row, 0, norm_v1 / math.sqrt(total_cols))
    row = put_lane(row, 1, norm_u1 / math.sqrt(total_rows))
    row = put_lane(row, 2, norm_v2 / math.sqrt(total_cols))
    row = put_lane(row, 3, norm_u2 / math.sqrt(total_rows))
    out_b[...] = row

    for copy in bulk:
        copy.wait_send()
    pltpu.make_async_copy(relayed, relayed, relay_sem.at[0]).wait()
    for index, span in drains:
        pltpu.make_async_copy(span, span, send.at[index]).wait()


def solution(mesh):
    nc, ns = mesh.shape["cell"], mesh.shape["station"]

    def per_device(sensitivity, tile_mask, data_panel, model_panel):
        rows, cols = sensitivity.shape
        kd, km = data_panel.shape[0], model_panel.shape[0]
        size = kd * nc
        tiles, halves = cols // LANES, rows // LANES
        own = tiles // ns
        vmem = pl.BlockSpec(memory_space=pltpu.VMEM)
        data_vector, model_vector, bidiag = pl.pallas_call(
            functools.partial(kernel, nc, ns, rows * ns, cols * nc),
            out_shape=(
                jax.ShapeDtypeStruct((halves, LANES), F32),
                jax.ShapeDtypeStruct((tiles, LANES), F32),
                jax.ShapeDtypeStruct((1, LANES), F32),
            ),
            in_specs=[
                pl.BlockSpec(memory_space=pl.ANY),
                pl.BlockSpec(memory_space=pltpu.SMEM),
                vmem,
                pl.BlockSpec(memory_space=pl.ANY),
            ],
            out_specs=(vmem, vmem, vmem),
            scratch_shapes=[
                pltpu.VMEM((rows, cols), F32),
                pltpu.VMEM((size, tiles, LANES), F32),
                pltpu.VMEM((size, own, LANES), F32),
                pltpu.VMEM((km, cols), F32),
                pltpu.VMEM((nc, halves * kd, LANES), F32),
                pltpu.VMEM((halves, size, LANES), F32),
                pltpu.VMEM((ns, size // 4, LANES), F32),
                pltpu.VMEM((nc, size // 4, LANES), F32),
                pltpu.VMEM((ns, size // 4, LANES), F32),
                pltpu.VMEM((2, tiles, LANES), F32),
                pltpu.VMEM((2, ns, own, LANES), F32),
                pltpu.VMEM((2, tiles, LANES), F32),
                pltpu.VMEM((2, nc, 1, LANES), F32),
                pltpu.VMEM((2, ns, 1, LANES), F32),
                pltpu.VMEM((2, tiles, LANES), F32),
                pltpu.VMEM((2, nc, halves + 2, LANES), F32),
                pltpu.VMEM((2, ns, 1, LANES), F32),
                pltpu.VMEM((ns, 1, LANES), F32),
                pltpu.VMEM((rows, LANES), F32),
                pltpu.VMEM((size, LANES), F32),
                pltpu.VMEM((size, LANES), F32),
                pltpu.SemaphoreType.DMA((9,)),
                pltpu.SemaphoreType.DMA((18,)),
                pltpu.SemaphoreType.DMA((18,)),
                pltpu.SemaphoreType.DMA((ns // 2,)),
                pltpu.SemaphoreType.DMA((2,)),
                pltpu.SemaphoreType.DMA((ns // 2,)),
            ],
            compiler_params=pltpu.CompilerParams(
                collective_id=0, has_side_effects=True, vmem_limit_bytes=48 * 1024 * 1024
            ),
            name="bidiagonalise",
        )(sensitivity, tile_mask, data_panel, model_panel)
        return data_vector.reshape(rows), model_vector.reshape(cols), bidiag[0, :4]

    return jax.shard_map(
        per_device,
        mesh=mesh,
        in_specs=(P("station", "cell"), P("station", "cell"), P("cell", "station"), P("station", "cell")),
        out_specs=(P("station"), P("cell"), P()),
        check_vma=False,
    )
```

time: 588 us -> 87.4 us (0.15)
  blocking collectives: 398 us -> 0 us
  Pallas kernels: 0 us -> 82.6 us
  matrix products: 67.1 us -> 0 us
  waiting for transfers between devices: 53 us -> 0 us
  other arithmetic: 29.7 us -> 0 us
  between operations: 16.9 us -> 0.65 us
  local copies, waits for them, and re-layouts: 18.1 us -> 4.01 us
    psum x12 -> x0, blocking collectives: 378 us -> none  [the longest x4 122 us: model_reduce(): return lax.psum(value, 'cell')]
    pallas_call x0 -> x1, Pallas kernels: none -> 82.6 us  [per_device(): pl.pallas_call(functools.partial(kernel, nc, ns, rows * ns, cols * nc), o...]
    dot_general x14 -> x0, matrix products: 63.4 us -> none  [the longest x2 32.1 us: forward_whole(): return lax.psum(jnp.dot(masked, vector, precision=HIGH), 'cell')]
    psum x2 -> x0, waiting for transfers between devices: 52.2 us -> none  [adjoint_whole(): return lax.psum(jnp.dot(vector, masked, precision=HIGH), 'station')]
    all_gather x1 -> x0, blocking collectives: 20 us -> none  [per_device(): data_full = lax.all_gather(data_panel, 'cell', axis=0, tiled=True)]
    another operation x11 -> x0, other arithmetic: 13.9 us -> none  [the longest x6 7.19 us: orthonormal(): lower = jnp.linalg.cholesky(gram)]
    mul x3 -> x0, other arithmetic: 12.6 us -> none  [the longest x1 11.3 us: per_device(): sensitivity.reshape(rows // TILE_ROWS, TILE_ROWS, cols // TILE_COLS, TILE...]
    unnamed x13 -> x8, local copies, waits for them, and re-layouts: 15.8 us -> 3.5 us
  transfers between devices with their start and end apart: 3 -> 0, of which waited for: 1 -> 0; matrix products, arithmetic and copies ran while one was open for 10% -> 0% of each run, Pallas kernels for 0% -> 0%
where the time goes in v1:
time: 87.4 us; the launch traced here: 87.2 us
  Pallas kernels  82.6 us (95%)
  local copies, waits for them, and re-layouts  4.01 us (5%)
    pallas_call x1, Pallas kernels, per_device(): pl.pallas_call(functools.partial(kernel, nc, ns, rows * ns, cols * nc), o...  82.6 us
    unnamed x8, local copies, waits for them, and re-layouts  3.5 us

profile of v1, /device:TPU:1, one launch (start us, length us, event | category | flops | bytes accessed | tf_op | source)
XLA Modules:
  0.0 87.2 jit_solution(3109680342304783086)
XLA Ops:
  0.6 0.0 copy-start
  0.6 0.9 %copy-done = f32[4,16384]{1,0:T(4,128)S(1)} copy-done((f32[4,16384]{1,0:T(4,128)S(1)}, f32[4,16384]{1,0:T(4,128)}, u32[]{:S(2)}) %copy-start) | copy-done | bytes 262168
  1.6 0.0 copy-start.1
  1.6 0.7 copy-done.1
  2.3 0.0 copy-start.2
  2.3 0.7 copy-done.2
  2.9 82.6 %bidiagonalise.1 = (f32[2,128]{1,0:T(2,128)S(1)}, f32[128,128]{1,0:T(8,128)S(1)}, f32[1,128]{1,0:T(1,128)S(1)}) custom-call(f32[256,16384]{1,0:T(8,128)} %sens.1, s32[2,32]{1,0:T(2,128)S(1)} %copy-done.2, f32[2,256]{1,0:T(2,128)S(1)} %copy-done.1, f32[4,16384]{1,0:T(4,128)S(1)} %copy-done), custom_call_target="tpu_custom_call" | custom-call | tf_op jit(solution)/shard_map/bidiagonalise/pallas_call | solution.py:370
  85.5 0.5 slice_bitcast_fusion
  86.0 0.6 copy.9
  86.6 0.6 copy.10
Async XLA Ops:
  0.6 1.0 %copy-start = (f32[4,16384]{1,0:T(4,128)S(1)}, f32[4,16384]{1,0:T(4,128)}, u32[]{:S(2)}) copy-start(f32[4,16384]{1,0:T(4,128)} %mp.1) | copy-start | bytes 786436
  1.6 0.7 copy-start.1
  2.3 0.7 copy-start.2

commit v2 on v1

v2 whole, which is shorter than its diff:
```python
import functools
import math

import jax
import jax.numpy as jnp
from jax import lax
from jax.experimental import pallas as pl
from jax.experimental.pallas import tpu as pltpu
from jax.sharding import PartitionSpec as P

TILE_ROWS = 128
TILE_COLS = 512
LANES = 128
HIGH = lax.Precision.HIGHEST
MESH = pl.DeviceIdType.MESH
F32 = jnp.float32


def eye_mask(rows):
    return lax.broadcasted_iota(jnp.int32, (rows, LANES), 0) == lax.broadcasted_iota(jnp.int32, (rows, LANES), 1)


def to_lanes(column, rows):
    return jnp.sum(jnp.where(eye_mask(rows), column, 0.0), axis=0, keepdims=True)


def to_rows(row, rows):
    return jnp.sum(jnp.where(eye_mask(rows), row, 0.0), axis=1, keepdims=True)


def lane(row, index):
    ids = lax.broadcasted_iota(jnp.int32, (1, LANES), 1)
    return jnp.sum(jnp.where(ids == index, row, 0.0), axis=1, keepdims=True)


def put_lane(row, index, value):
    ids = lax.broadcasted_iota(jnp.int32, (1, LANES), 1)
    return jnp.where(ids == index, value, row)


def total(x):
    return jnp.sum(jnp.sum(x, axis=0, keepdims=True), axis=1, keepdims=True)


def dot_t(a, b):
    return lax.dot_general(a, b, (((1,), (1,)), ((), ())), precision=HIGH, preferred_element_type=F32)


def pack(gram):
    rows = gram.shape[0] // 4
    return jnp.concatenate([gram[q * rows : (q + 1) * rows, :] for q in range(4)], axis=1)


def unpack(packed, size):
    return jnp.concatenate([packed[:, q * size : (q + 1) * size] for q in range(4)], axis=0)


def inverse(gram, size):
    rows = lax.broadcasted_iota(jnp.int32, (size, LANES), 0)
    unit = jnp.where(
        rows + size == lax.broadcasted_iota(jnp.int32, (size, LANES), 1), 1.0, 0.0
    )
    a = jnp.concatenate([gram, jnp.zeros((size, LANES - size), F32)], axis=1) + unit
    for i in range(size):
        pivot_row = a[i : i + 1, :] / a[i : i + 1, i : i + 1]
        a = jnp.where(rows == i, pivot_row, a - a[:, i : i + 1] * pivot_row)
    return jnp.concatenate([a[:, size : 2 * size], jnp.zeros((size, LANES - size), F32)], axis=1)


def kernel(
    nc, ns, total_rows, total_cols,
    sens, mask_in, dp_in, mp,
    out_u, out_v, out_b,
    g, pfull, pown, plocal, mask, dp, dloc, d1, ds, puc, pud, gu, gmc, gms,
    wpart, rs, ag, ca, rbuf, nv, fa, ubuf, ub, stack, ybuf,
    load_sem, send, recv, bulk_send, bulk_recv,
):
    me_c, me_s = lax.axis_index("cell"), lax.axis_index("station")
    nz, nx = ns // 2, min(nc, 4)
    ny = nc // nx
    me = me_c * ns + me_s
    z, core = me_s // 2, me_s % 2
    y, x = me_c // nx, me_c % nx
    rows, cols = sens.shape
    tiles = cols // LANES
    own = tiles // ns
    kd, km = dp.shape[0], mp.shape[0]
    size = kd * nc
    halves = rows // LANES
    per = TILE_COLS // LANES

    load_rows = rows // 8
    loads = [
        pltpu.make_async_copy(
            sens.at[pl.ds(q * load_rows, load_rows), :], g.at[pl.ds(q * load_rows, load_rows), :], load_sem.at[q]
        )
        for q in range(8)
    ]
    load_dp = pltpu.make_async_copy(dp_in, dp, load_sem.at[8])
    load_mp = pltpu.make_async_copy(mp, plocal, load_sem.at[9])
    load_mask = pltpu.make_async_copy(mask_in, mask, load_sem.at[10])

    def far(n):
        return sorted(range(n), key=lambda d: -min(d, n - d))

    cells = [((y + dy) % ny) * nx + (x + dx) % nx for dy in far(ny) for dx in far(nx)]
    stations = [((z + dz) % nz) * 2 + (core + dk) % 2 for dz in far(nz) for dk in (1, 0)]
    cell_peers, station_peers = cells[:-1], stations[:-1]

    barrier = pltpu.get_barrier_semaphore()
    for peer in cell_peers:
        pl.semaphore_signal(barrier, inc=1, device_id={"cell": peer}, device_id_type=MESH)
    for peer in station_peers:
        pl.semaphore_signal(barrier, inc=1, device_id={"station": peer}, device_id_type=MESH)
    for copy in [load_dp, load_mp, load_mask, *loads]:
        copy.start()

    drains = []

    def remote(src, dst, send_sem, recv_sem, where):
        return pltpu.make_async_remote_copy(
            src_ref=src, dst_ref=dst, send_sem=send_sem, recv_sem=recv_sem, device_id=where, device_id_type=MESH
        )

    def exchange(axis, src, dst, index):
        for peer in cell_peers if axis == "cell" else station_peers:
            remote(src(peer), dst, send.at[index], recv.at[index], {axis: peer}).start()

    def exchange_all(src, dst, index):
        for i, c in enumerate(cells):
            for s in stations if i < nc - 1 else station_peers:
                remote(src, dst, send.at[index], recv.at[index], {"cell": c, "station": s}).start()

    def wait_all(index, span):
        pltpu.make_async_copy(span, span, recv.at[index]).wait()
        drains.append((index, span))

    load_dp.wait()
    block = dp[...]
    for h in range(halves):
        dloc[h] = block[:, h * LANES : (h + 1) * LANES]
    d1[me_c] = dloc[...]
    ds[me_s] = dloc[...]

    load_mp.wait()

    @pl.loop(0, tiles)
    def _(j):
        piece = plocal[:, pl.ds(pl.multiple_of(j * LANES, LANES), LANES)]
        for k in range(km):
            pfull[me_s * km + k, pl.ds(j, 1), :] = piece[k : k + 1, :]

    mine = pl.ds(me_s * km, km)
    pown[mine, :, :] = pfull[mine, pl.ds(pl.multiple_of(me_s * own, own), own), :]
    pl.semaphore_wait(barrier, nc + ns - 2)

    exchange("cell", lambda peer: dloc, d1.at[me_c], 0)
    exchange("station", lambda peer: dloc, ds.at[me_s], 1)
    exchange(
        "station",
        lambda peer: pfull.at[mine, pl.ds(pl.multiple_of(peer * own, own), own), :],
        pown.at[mine, :, :],
        2,
    )
    up, down, partner = ((z + 1) % nz) * 2 + core, ((z + nz - 1) % nz) * 2 + core, z * 2 + 1 - core
    across = ((z + 2) % nz) * 2 + core
    half = tiles // 2
    bulk = {}

    def pass_on(who, at, index, target):
        view = pfull.at[pl.ds(who * km, km), at, :]
        copy = remote(view, view, bulk_send.at[index], bulk_recv.at[index], {"station": target})
        copy.start()
        bulk[index] = copy

    everything, low, high = pl.ds(0, tiles), pl.ds(0, half), pl.ds(half, half)

    def bulk_start():
        pass_on(me_s, everything, 0, up)
        pass_on(me_s, everything, 1, down)
        pass_on(me_s, everything, 2, partner)

    def bulk_relay():
        bulk[0].wait_recv()
        pass_on(down, low, 3, up)
        pass_on(down, everything, 5, partner)
        bulk[1].wait_recv()
        pass_on(up, high, 4, down)
        pass_on(up, everything, 6, partner)

    def bulk_last():
        bulk[3].wait_recv()
        pass_on(across, low, 7, partner)
        bulk[4].wait_recv()
        pass_on(across, high, 8, partner)

    def bulk_finish():
        for i in (2, 5, 6, 7, 8):
            bulk[i].wait_recv()


    wait_all(0, d1.at[pl.ds(0, nc - 1)])
    p64 = []
    for h in range(halves):
        for c in range(nc):
            pud[me_s * halves + h, c * kd : (c + 1) * kd, :] = d1[c, h]
        p64.append(pud[me_s * halves + h])
    gram = dot_t(p64[0], p64[0])
    for h in range(1, halves):
        gram = gram + dot_t(p64[h], p64[h])
    gu[me_s] = pack(gram)
    exchange("station", lambda peer: gu.at[me_s], gu.at[me_s], 3)

    wait_all(1, ds.at[pl.ds(0, ns - 1)])
    puc[:, :, me_c] = ds[...]
    exchange("cell", lambda peer: ds, puc.at[:, :, me_c], 4)

    wait_all(2, pown.at[pl.ds(0, km * (ns - 1))])
    mine_all = jnp.concatenate([pown[:, j, :] for j in range(own)], axis=1)
    gmc[me_c] = pack(dot_t(mine_all, mine_all))
    exchange("cell", lambda peer: gmc.at[me_c], gmc.at[me_c], 5)

    wait_all(3, gu.at[pl.ds(0, ns - 1)])
    bulk_start()
    t_u = inverse(unpack(jnp.sum(gu[...], axis=0), size), size)
    x_col = t_u[:, size - 1 : size] / jnp.sqrt(t_u[size - 1 : size, size - 1 : size])
    start = [jnp.sum(x_col * p64[h], axis=0, keepdims=True) for h in range(halves)]

    wait_all(5, gmc.at[pl.ds(0, nc - 1)])
    gms[me_s] = jnp.sum(gmc[...], axis=0)
    exchange("station", lambda peer: gms.at[me_s], gms.at[me_s], 6)
    load_mask.wait()
    for copy in loads:
        copy.wait()

    def adjoint(vector, t):
        for h in range(halves):
            ub[h * LANES : (h + 1) * LANES, :] = jnp.broadcast_to(to_rows(vector[h], LANES), (LANES, LANES))

        @pl.loop(0, tiles // per)
        def _(j):
            for q in range(per):
                at = pl.ds(pl.multiple_of((j * per + q) * LANES, LANES), LANES)
                result = None
                for h in range(halves):
                    parts = [None, None]
                    for r in range(h * LANES, (h + 1) * LANES, 8):
                        term = g[r : r + 8, at] * ub[r : r + 8, :]
                        w = (r // 8) % 2
                        parts[w] = term if parts[w] is None else parts[w] + term
                    part = (parts[0] + parts[1]) * mask[h, j].astype(F32)
                    result = part if result is None else result + part
                wpart[t, pl.ds(j * per + q, 1), :] = jnp.sum(result, axis=0, keepdims=True)

    def forward(t):
        def step(j, sums):
            sums = list(sums)
            for q in range(per):
                at = pl.ds(pl.multiple_of((j * per + q) * LANES, LANES), LANES)
                row = rbuf[t, pl.ds(j * per + q, 1), :]
                for h in range(halves):
                    sums[h] = sums[h] + g[h * LANES : (h + 1) * LANES, at] * (row * mask[h, j].astype(F32))
            return tuple(sums)

        sums = lax.fori_loop(0, tiles // per, step, tuple(jnp.zeros((LANES, LANES), F32) for _ in range(halves)))
        return [to_lanes(jnp.sum(part, axis=1, keepdims=True), LANES) for part in sums]

    own_at = pl.ds(pl.multiple_of(me_s * own, own), own)

    def scatter(t, index):
        rs[t, me_s] = wpart[t, own_at, :]
        exchange(
            "station",
            lambda peer: wpart.at[t, pl.ds(pl.multiple_of(peer * own, own), own), :],
            rs.at[t, me_s],
            index,
        )

    def gather(t, index_rs, index_ag):
        wait_all(index_rs, rs.at[t, pl.ds(0, ns - 1)])
        w_own = jnp.sum(rs[t], axis=0)
        ag[t, own_at, :] = w_own
        exchange("station", lambda peer: ag.at[t, own_at, :], ag.at[t, own_at, :], index_ag)
        return w_own

    def share_coef(t, coef, index):
        ca[t, me] = coef
        exchange_all(ca.at[t, me], ca.at[t, me], index)

    def summed_coef(t, index):
        wait_all(index, ca.at[t, pl.ds(0, nc * ns - 1)])
        return jnp.sum(ca[t], axis=0)

    def reorthogonalise(t, w, coef, extra, index):
        y = jnp.sum(t_m * coef, axis=1, keepdims=True)
        ybuf[...] = jnp.broadcast_to(y, (size, LANES))
        rest = w if extra is None else w - extra

        def step(k, rest):
            return rest - pfull[k] * ybuf[pl.ds(k, 1), :]

        rest = lax.fori_loop(0, size, step, rest, unroll=4)
        rbuf[t] = rest
        nv[t, me_c] = jnp.broadcast_to(total(rest * rest), (1, LANES))
        exchange("cell", lambda peer: nv.at[t, me_c], nv.at[t, me_c], index)

    def data_side(t, index_nv, index_fa, before):
        parts = forward(t)
        for h in range(halves):
            fa[t, me, h : h + 1, :] = parts[h]
        exchange_all(fa.at[t, me], fa.at[t, me], index_fa)
        wait_all(index_nv, nv.at[t, pl.ds(0, nc - 1)])
        norm_v = jnp.sqrt(jnp.sum(nv[t], axis=0)[:, 0:1])
        scale = 1.0 / norm_v
        wait_all(index_fa, fa.at[t, pl.ds(0, nc * ns - 1)])
        for s in range(ns):
            piece = fa[t, s]
            for c in range(1, nc):
                piece = piece + fa[t, c * ns + s]
            ubuf[s * halves : (s + 1) * halves, :] = piece * scale
        vec = ubuf[...]
        count = ns * halves
        col = pud[0] * vec[0:1, :]
        for i in range(1, count):
            col = col + pud[i] * vec[i : i + 1, :]
        coef = to_lanes(jnp.sum(col, axis=1, keepdims=True), size)
        y = jnp.sum(t_u * coef, axis=1, keepdims=True)
        rest = vec
        if before is not None:
            rest = rest - before * total(before * vec)
        for i in range(count):
            ubuf[i : i + 1, :] = jnp.sum(y * pud[i], axis=0, keepdims=True)
        rest = rest - ubuf[...]
        norm_u = jnp.sqrt(total(rest * rest))
        rest = rest / norm_u
        ubuf[...] = rest
        mine_u = [ubuf[pl.ds(me_s * halves + h, 1), :] for h in range(halves)]
        return rest, mine_u, norm_u, norm_v, scale

    adjoint(start, 0)
    scatter(0, 7)
    bulk_relay()
    w_own = gather(0, 7, 8)
    for k in range(size):
        stack[k : k + 1, :] = jnp.sum(pown[k] * w_own, axis=0, keepdims=True)
    share_coef(0, to_lanes(jnp.sum(stack[...], axis=1, keepdims=True), size), 9)
    wait_all(6, gms.at[pl.ds(0, ns - 1)])
    t_m = inverse(unpack(jnp.sum(gms[...], axis=0), size), size)
    bulk_last()
    wait_all(4, puc.at[:, :, pl.ds(0, nc - 1)])
    for s in range(ns):
        for h in range(halves):
            for c in range(nc):
                pud[s * halves + h, c * kd : (c + 1) * kd, :] = puc[s, h, c]
    wait_all(8, ag.at[0, pl.ds(0, own * (ns - 1)), :])
    coef = summed_coef(0, 9)
    bulk_finish()
    reorthogonalise(0, ag[0], coef, None, 10)
    first_u, mine_u, norm_u1, norm_v1, scale_v1 = data_side(0, 10, 11, None)

    adjoint(mine_u, 1)
    scatter(1, 12)
    part = wpart[1]

    def step(k, carry):
        stack[pl.ds(k, 1), :] = jnp.sum(pfull[k] * part, axis=0, keepdims=True)
        return carry

    lax.fori_loop(0, size, step, 0, unroll=4)
    coef = to_lanes(jnp.sum(stack[...], axis=1, keepdims=True), size)
    share_coef(1, put_lane(coef, size, total(rbuf[0] * part) * scale_v1), 13)
    gather(1, 12, 14)
    coef = summed_coef(1, 13)
    along = rbuf[0] * (lane(coef, size) * scale_v1)
    wait_all(14, ag.at[1, pl.ds(0, own * (ns - 1)), :])
    reorthogonalise(1, ag[1], coef, along, 15)
    second_u, mine_u, norm_u2, norm_v2, scale_v2 = data_side(1, 15, 16, first_u)

    out_v[...] = rbuf[1] * (scale_v2 * math.sqrt(total_cols))
    for h in range(halves):
        out_u[h : h + 1, :] = mine_u[h] * math.sqrt(total_rows)
    row = jnp.zeros((1, LANES), F32)
    row = put_lane(row, 0, norm_v1 / math.sqrt(total_cols))
    row = put_lane(row, 1, norm_u1 / math.sqrt(total_rows))
    row = put_lane(row, 2, norm_v2 / math.sqrt(total_cols))
    row = put_lane(row, 3, norm_u2 / math.sqrt(total_rows))
    out_b[...] = row

    for copy in bulk.values():
        copy.wait_send()
    for index, span in drains:
        pltpu.make_async_copy(span, span, send.at[index]).wait()


def solution(mesh):
    nc, ns = mesh.shape["cell"], mesh.shape["station"]

    def per_device(sensitivity, tile_mask, data_panel, model_panel):
        rows, cols = sensitivity.shape
        kd, km = data_panel.shape[0], model_panel.shape[0]
        size = kd * nc
        tiles, halves = cols // LANES, rows // LANES
        own = tiles // ns
        vmem = pl.BlockSpec(memory_space=pltpu.VMEM)
        data_vector, model_vector, bidiag = pl.pallas_call(
            functools.partial(kernel, nc, ns, rows * ns, cols * nc),
            out_shape=(
                jax.ShapeDtypeStruct((halves, LANES), F32),
                jax.ShapeDtypeStruct((tiles, LANES), F32),
                jax.ShapeDtypeStruct((1, LANES), F32),
            ),
            in_specs=[pl.BlockSpec(memory_space=pltpu.HBM)] * 4,
            out_specs=(vmem, vmem, vmem),
            scratch_shapes=[
                pltpu.VMEM((rows, cols), F32),
                pltpu.VMEM((size, tiles, LANES), F32),
                pltpu.VMEM((size, own, LANES), F32),
                pltpu.VMEM((km, cols), F32),
                pltpu.SMEM(tile_mask.shape, jnp.int32),
                pltpu.VMEM(data_panel.shape, F32),
                pltpu.VMEM((halves, kd, LANES), F32),
                pltpu.VMEM((nc, halves, kd, LANES), F32),
                pltpu.VMEM((ns, halves, kd, LANES), F32),
                pltpu.VMEM((ns, halves, nc, kd, LANES), F32),
                pltpu.VMEM((ns * halves, size, LANES), F32),
                pltpu.VMEM((ns, size // 4, LANES), F32),
                pltpu.VMEM((nc, size // 4, LANES), F32),
                pltpu.VMEM((ns, size // 4, LANES), F32),
                pltpu.VMEM((2, tiles, LANES), F32),
                pltpu.VMEM((2, ns, own, LANES), F32),
                pltpu.VMEM((2, tiles, LANES), F32),
                pltpu.VMEM((2, nc * ns, 1, LANES), F32),
                pltpu.VMEM((2, tiles, LANES), F32),
                pltpu.VMEM((2, nc, 1, LANES), F32),
                pltpu.VMEM((2, nc * ns, halves, LANES), F32),
                pltpu.VMEM((ns * halves, LANES), F32),
                pltpu.VMEM((rows, LANES), F32),
                pltpu.VMEM((size, LANES), F32),
                pltpu.VMEM((size, LANES), F32),
                pltpu.SemaphoreType.DMA((11,)),
                pltpu.SemaphoreType.DMA((17,)),
                pltpu.SemaphoreType.DMA((17,)),
                pltpu.SemaphoreType.DMA((9,)),
                pltpu.SemaphoreType.DMA((9,)),
            ],
            compiler_params=pltpu.CompilerParams(
                collective_id=0, has_side_effects=True, vmem_limit_bytes=48 * 1024 * 1024
            ),
            name="bidiagonalise",
        )(sensitivity, tile_mask, data_panel, model_panel)
        return data_vector.reshape(rows), model_vector.reshape(cols), bidiag[0, :4]

    return jax.shard_map(
        per_device,
        mesh=mesh,
        in_specs=(P("station", "cell"), P("station", "cell"), P("cell", "station"), P("station", "cell")),
        out_specs=(P("station"), P("cell"), P()),
        check_vma=False,
    )
```

time: 87.4 us -> 67.2 us (0.77)
  Pallas kernels: 82.6 us -> 62.3 us
    pallas_call x1, Pallas kernels: 82.6 us -> 62.3 us  [per_device(): pl.pallas_call(functools.partial(kernel, nc, ns, rows * ns, cols * nc), o...]
where the time goes in v2:
time: 67.2 us; the launch traced here: 67 us
  Pallas kernels  62.3 us (93%)
  local copies, waits for them, and re-layouts  4.01 us (6%)
    pallas_call x1, Pallas kernels, per_device(): pl.pallas_call(functools.partial(kernel, nc, ns, rows * ns, cols * nc), o...  62.3 us
    unnamed x8, local copies, waits for them, and re-layouts  3.5 us

profile of v2, /device:TPU:1, one launch (start us, length us, event | category | flops | bytes accessed | tf_op | source)
XLA Modules:
  0.0 67.0 jit_solution(1468589844890617112)
XLA Ops:
  0.6 0.0 copy-start
  0.6 0.9 %copy-done = f32[4,16384]{1,0:T(4,128)S(1)} copy-done((f32[4,16384]{1,0:T(4,128)S(1)}, f32[4,16384]{1,0:T(4,128)}, u32[]{:S(2)}) %copy-start) | copy-done | bytes 262168
  1.6 0.0 copy-start.1
  1.6 0.7 %copy-done.1 = f32[2,256]{1,0:T(2,128)S(1)} copy-done((f32[2,256]{1,0:T(2,128)S(1)}, f32[2,256]{1,0:T(2,128)}, u32[]{:S(2)}) %copy-start.1) | copy-done | bytes 2072
  2.3 0.0 copy-start.2
  2.3 0.7 %copy-done.2 = s32[2,32]{1,0:T(2,128)S(1)} copy-done((s32[2,32]{1,0:T(2,128)S(1)}, s32[2,32]{1,0:T(2,128)}, u32[]{:S(2)}) %copy-start.2) | copy-done | bytes 280
  2.9 62.3 %bidiagonalise.1 = (f32[2,128]{1,0:T(2,128)S(1)}, f32[128,128]{1,0:T(8,128)S(1)}, f32[1,128]{1,0:T(1,128)S(1)}) custom-call(f32[256,16384]{1,0:T(8,128)} %sens.1, s32[2,32]{1,0:T(2,128)S(1)} %copy-done.2, f32[2,256]{1,0:T(2,128)S(1)} %copy-done.1, f32[4,16384]{1,0:T(4,128)S(1)} %copy-done), custom_call_target="tpu_custom_call" | custom-call | tf_op jit(solution)/shard_map/bidiagonalise/pallas_call | solution.py:405
  65.3 0.5 slice_bitcast_fusion
  65.8 0.6 copy.9
  66.4 0.6 copy.10
Async XLA Ops:
  0.6 1.0 %copy-start = (f32[4,16384]{1,0:T(4,128)S(1)}, f32[4,16384]{1,0:T(4,128)}, u32[]{:S(2)}) copy-start(f32[4,16384]{1,0:T(4,128)} %mp.1) | copy-start | bytes 786436
  1.6 0.7 %copy-start.1 = (f32[2,256]{1,0:T(2,128)S(1)}, f32[2,256]{1,0:T(2,128)}, u32[]{:S(2)}) copy-start(f32[2,256]{1,0:T(2,128)} %dp_in.1) | copy-start | bytes 6148
  2.3 0.7 %copy-start.2 = (s32[2,32]{1,0:T(2,128)S(1)}, s32[2,32]{1,0:T(2,128)}, u32[]{:S(2)}) copy-start(s32[2,32]{1,0:T(2,128)} %mask_in.1) | copy-start | bytes 772

commit v3 on v2

--- a/solution.py
+++ b/solution.py
@@ -61,9 +61,13 @@
         rows + size == lax.broadcasted_iota(jnp.int32, (size, LANES), 1), 1.0, 0.0
     )
     a = jnp.concatenate([gram, jnp.zeros((size, LANES - size), F32)], axis=1) + unit
-    for i in range(size):
-        pivot_row = a[i : i + 1, :] / a[i : i + 1, i : i + 1]
-        a = jnp.where(rows == i, pivot_row, a - a[:, i : i + 1] * pivot_row)
+    for i in range(0, size, 2):
+        r0, r1 = a[i : i + 1, :], a[i + 1 : i + 2, :]
+        p, q, r = r0[:, i : i + 1], r0[:, i + 1 : i + 2], r1[:, i + 1 : i + 2]
+        scale = 1.0 / (p * r - q * q)
+        new0, new1 = (r * scale) * r0 - (q * scale) * r1, (p * scale) * r1 - (q * scale) * r0
+        rest = a - a[:, i : i + 1] * new0 - a[:, i + 1 : i + 2] * new1
+        a = jnp.where(rows == i, new0, jnp.where(rows == i + 1, new1, rest))
     return jnp.concatenate([a[:, size : 2 * size], jnp.zeros((size, LANES - size), F32)], axis=1)
 
 
@@ -72,7 +76,7 @@
     sens, mask_in, dp_in, mp,
     out_u, out_v, out_b,
     g, pfull, pown, plocal, mask, dp, dloc, d1, ds, puc, pud, gu, gmc, gms,
-    wpart, rs, ag, ca, rbuf, nv, fa, ubuf, ub, stack, ybuf,
+    wpart, rs, ag, ca, rbuf, nv, fa, ubuf, ub, stack, parts, ybuf,
     load_sem, send, recv, bulk_send, bulk_recv,
 ):
     me_c, me_s = lax.axis_index("cell"), lax.axis_index("station")
@@ -89,16 +93,13 @@
     halves = rows // LANES
     per = TILE_COLS // LANES
 
-    load_rows = rows // 8
+    width = cols // ns
     loads = [
-        pltpu.make_async_copy(
-            sens.at[pl.ds(q * load_rows, load_rows), :], g.at[pl.ds(q * load_rows, load_rows), :], load_sem.at[q]
-        )
-        for q in range(8)
+        pltpu.make_async_copy(sens.at[:, pl.ds(q * width, width)], g.at[q], load_sem.at[q]) for q in range(ns)
     ]
-    load_dp = pltpu.make_async_copy(dp_in, dp, load_sem.at[8])
-    load_mp = pltpu.make_async_copy(mp, plocal, load_sem.at[9])
-    load_mask = pltpu.make_async_copy(mask_in, mask, load_sem.at[10])
+    load_dp = pltpu.make_async_copy(dp_in, dp, load_sem.at[ns])
+    load_mp = pltpu.make_async_copy(mp, plocal, load_sem.at[ns + 1])
+    load_mask = pltpu.make_async_copy(mask_in, mask, load_sem.at[ns + 2])
 
     def far(n):
         return sorted(range(n), key=lambda d: -min(d, n - d))
@@ -210,6 +211,7 @@
         gram = gram + dot_t(p64[h], p64[h])
     gu[me_s] = pack(gram)
     exchange("station", lambda peer: gu.at[me_s], gu.at[me_s], 3)
+    bulk_start()
 
     wait_all(1, ds.at[pl.ds(0, ns - 1)])
     puc[:, :, me_c] = ds[...]
@@ -221,7 +223,6 @@
     exchange("cell", lambda peer: gmc.at[me_c], gmc.at[me_c], 5)
 
     wait_all(3, gu.at[pl.ds(0, ns - 1)])
-    bulk_start()
     t_u = inverse(unpack(jnp.sum(gu[...], axis=0), size), size)
     x_col = t_u[:, size - 1 : size] / jnp.sqrt(t_u[size - 1 : size, size - 1 : size])
     start = [jnp.sum(x_col * p64[h], axis=0, keepdims=True) for h in range(halves)]
@@ -233,48 +234,49 @@
     for copy in loads:
         copy.wait()
 
-    def adjoint(vector, t):
+    def adjoint(vector, t, index):
         for h in range(halves):
             ub[h * LANES : (h + 1) * LANES, :] = jnp.broadcast_to(to_rows(vector[h], LANES), (LANES, LANES))
-
-        @pl.loop(0, tiles // per)
-        def _(j):
-            for q in range(per):
-                at = pl.ds(pl.multiple_of((j * per + q) * LANES, LANES), LANES)
-                result = None
-                for h in range(halves):
-                    parts = [None, None]
-                    for r in range(h * LANES, (h + 1) * LANES, 8):
-                        term = g[r : r + 8, at] * ub[r : r + 8, :]
-                        w = (r // 8) % 2
-                        parts[w] = term if parts[w] is None else parts[w] + term
-                    part = (parts[0] + parts[1]) * mask[h, j].astype(F32)
-                    result = part if result is None else result + part
-                wpart[t, pl.ds(j * per + q, 1), :] = jnp.sum(result, axis=0, keepdims=True)
+        for s in stations:
+            for h in range(halves):
+                u = ub[h * LANES : (h + 1) * LANES, :]
+                for i in range(own):
+                    product = g[s, h * LANES : (h + 1) * LANES, i * LANES : (i + 1) * LANES] * u
+                    part = jnp.sum(product.reshape(LANES // 8, 8, LANES), axis=0)
+                    part = part * mask[h, s * (own // per) + i // per].astype(F32)
+                    if h > 0:
+                        part = part + parts[i]
+                    if h < halves - 1:
+                        parts[i] = part
+                    else:
+                        wpart[t, pl.ds(s * own + i, 1), :] = jnp.sum(part, axis=0, keepdims=True)
+            there = pl.ds(pl.multiple_of(s * own, own), own)
+            if s is stations[-1]:
+                rs[t, me_s] = wpart[t, there, :]
+            else:
+                remote(wpart.at[t, there, :], rs.at[t, me_s], send.at[index], recv.at[index], {"station": s}).start()
 
     def forward(t):
-        def step(j, sums):
-            sums = list(sums)
-            for q in range(per):
-                at = pl.ds(pl.multiple_of((j * per + q) * LANES, LANES), LANES)
-                row = rbuf[t, pl.ds(j * per + q, 1), :]
-                for h in range(halves):
-                    sums[h] = sums[h] + g[h * LANES : (h + 1) * LANES, at] * (row * mask[h, j].astype(F32))
-            return tuple(sums)
-
-        sums = lax.fori_loop(0, tiles // per, step, tuple(jnp.zeros((LANES, LANES), F32) for _ in range(halves)))
-        return [to_lanes(jnp.sum(part, axis=1, keepdims=True), LANES) for part in sums]
+        result = []
+        for h in range(halves):
+
+            def step(s, total_h):
+                for i in range(own):
+                    row = rbuf[t, pl.ds(s * own + i, 1), :] * mask[h, s * (own // per) + i // per].astype(F32)
+                    total_h = total_h + g[s, h * LANES : (h + 1) * LANES, i * LANES : (i + 1) * LANES] * row
+                return total_h
+
+            total_h = lax.fori_loop(0, ns, step, jnp.zeros((LANES, LANES), F32))
+            result.append(to_lanes(jnp.sum(total_h, axis=1, keepdims=True), LANES))
+        return result
 
     own_at = pl.ds(pl.multiple_of(me_s * own, own), own)
 
-    def scatter(t, index):
-        rs[t, me_s] = wpart[t, own_at, :]
-        exchange(
-            "station",
-            lambda peer: wpart.at[t, pl.ds(pl.multiple_of(peer * own, own), own), :],
-            rs.at[t, me_s],
-            index,
-        )
+    def panel_coef(panel, vector):
+        for k in range(size):
+            product = panel[k] * vector
+            stack[k] = jnp.sum(product.reshape(product.shape[0] // 8, 8, LANES), axis=0)
+        return to_lanes(jnp.sum(jnp.sum(stack[...], axis=1), axis=1, keepdims=True), size)
 
     def gather(t, index_rs, index_ag):
         wait_all(index_rs, rs.at[t, pl.ds(0, ns - 1)])
@@ -295,11 +297,8 @@
         y = jnp.sum(t_m * coef, axis=1, keepdims=True)
         ybuf[...] = jnp.broadcast_to(y, (size, LANES))
         rest = w if extra is None else w - extra
-
-        def step(k, rest):
-            return rest - pfull[k] * ybuf[pl.ds(k, 1), :]
-
-        rest = lax.fori_loop(0, size, step, rest, unroll=4)
+        for k in range(size):
+            rest = rest - pfull[k] * ybuf[k : k + 1, :]
         rbuf[t] = rest
         nv[t, me_c] = jnp.broadcast_to(total(rest * rest), (1, LANES))
         exchange("cell", lambda peer: nv.at[t, me_c], nv.at[t, me_c], index)
@@ -337,13 +336,10 @@
         mine_u = [ubuf[pl.ds(me_s * halves + h, 1), :] for h in range(halves)]
         return rest, mine_u, norm_u, norm_v, scale
 
-    adjoint(start, 0)
-    scatter(0, 7)
+    adjoint(start, 0, 7)
     bulk_relay()
     w_own = gather(0, 7, 8)
-    for k in range(size):
-        stack[k : k + 1, :] = jnp.sum(pown[k] * w_own, axis=0, keepdims=True)
-    share_coef(0, to_lanes(jnp.sum(stack[...], axis=1, keepdims=True), size), 9)
+    share_coef(0, panel_coef(pown, w_own), 9)
     wait_all(6, gms.at[pl.ds(0, ns - 1)])
     t_m = inverse(unpack(jnp.sum(gms[...], axis=0), size), size)
     bulk_last()
@@ -358,16 +354,9 @@
     reorthogonalise(0, ag[0], coef, None, 10)
     first_u, mine_u, norm_u1, norm_v1, scale_v1 = data_side(0, 10, 11, None)
 
-    adjoint(mine_u, 1)
-    scatter(1, 12)
+    adjoint(mine_u, 1, 12)
     part = wpart[1]
-
-    def step(k, carry):
-        stack[pl.ds(k, 1), :] = jnp.sum(pfull[k] * part, axis=0, keepdims=True)
-        return carry
-
-    lax.fori_loop(0, size, step, 0, unroll=4)
-    coef = to_lanes(jnp.sum(stack[...], axis=1, keepdims=True), size)
+    coef = panel_coef(pfull, part)
     share_coef(1, put_lane(coef, size, total(rbuf[0] * part) * scale_v1), 13)
     gather(1, 12, 14)
     coef = summed_coef(1, 13)
@@ -412,7 +401,7 @@
             in_specs=[pl.BlockSpec(memory_space=pltpu.HBM)] * 4,
             out_specs=(vmem, vmem, vmem),
             scratch_shapes=[
-                pltpu.VMEM((rows, cols), F32),
+                pltpu.VMEM((ns, rows, cols // ns), F32),
                 pltpu.VMEM((size, tiles, LANES), F32),
                 pltpu.VMEM((size, own, LANES), F32),
                 pltpu.VMEM((km, cols), F32),
@@ -435,9 +424,10 @@
                 pltpu.VMEM((2, nc * ns, halves, LANES), F32),
                 pltpu.VMEM((ns * halves, LANES), F32),
                 pltpu.VMEM((rows, LANES), F32),
+                pltpu.VMEM((size, 8, LANES), F32),
+                pltpu.VMEM((own, 8, LANES), F32),
                 pltpu.VMEM((size, LANES), F32),
-                pltpu.VMEM((size, LANES), F32),
-                pltpu.SemaphoreType.DMA((11,)),
+                pltpu.SemaphoreType.DMA((ns + 3,)),
                 pltpu.SemaphoreType.DMA((17,)),
                 pltpu.SemaphoreType.DMA((17,)),
                 pltpu.SemaphoreType.DMA((9,)),

time: 67.2 us -> 60.7 us (0.903)
  Pallas kernels: 62.3 us -> 55.9 us
    pallas_call x1, Pallas kernels: 62.3 us -> 55.9 us  [per_device(): pl.pallas_call(functools.partial(kernel, nc, ns, rows * ns, cols * nc), o...]
where the time goes in v3:
time: 60.7 us; the launch traced here: 60.5 us
  Pallas kernels  55.9 us (92%)
  local copies, waits for them, and re-layouts  4.01 us (7%)
  between operations  0.65 us (1%)
    pallas_call x1, Pallas kernels, per_device(): pl.pallas_call(functools.partial(kernel, nc, ns, rows * ns, cols * nc), o...  55.9 us
    unnamed x8, local copies, waits for them, and re-layouts  3.5 us

profile of v3, /device:TPU:1, one launch (start us, length us, event | category | flops | bytes accessed | tf_op | source)
XLA Modules:
  0.0 60.5 jit_solution(13884377239029758516)
XLA Ops:
  0.6 0.0 copy-start
  0.6 0.9 %copy-done = f32[4,16384]{1,0:T(4,128)S(1)} copy-done((f32[4,16384]{1,0:T(4,128)S(1)}, f32[4,16384]{1,0:T(4,128)}, u32[]{:S(2)}) %copy-start) | copy-done | bytes 262168
  1.6 0.0 copy-start.1
  1.6 0.7 %copy-done.1 = f32[2,256]{1,0:T(2,128)S(1)} copy-done((f32[2,256]{1,0:T(2,128)S(1)}, f32[2,256]{1,0:T(2,128)}, u32[]{:S(2)}) %copy-start.1) | copy-done | bytes 2072
  2.3 0.0 copy-start.2
  2.3 0.7 %copy-done.2 = s32[2,32]{1,0:T(2,128)S(1)} copy-done((s32[2,32]{1,0:T(2,128)S(1)}, s32[2,32]{1,0:T(2,128)}, u32[]{:S(2)}) %copy-start.2) | copy-done | bytes 280
  2.9 55.9 %bidiagonalise.1 = (f32[2,128]{1,0:T(2,128)S(1)}, f32[128,128]{1,0:T(8,128)S(1)}, f32[1,128]{1,0:T(1,128)S(1)}) custom-call(f32[256,16384]{1,0:T(8,128)} %sens.1, s32[2,32]{1,0:T(2,128)S(1)} %copy-done.2, f32[2,256]{1,0:T(2,128)S(1)} %copy-done.1, f32[4,16384]{1,0:T(4,128)S(1)} %copy-done), custom_call_target="tpu_custom_call" | custom-call | tf_op jit(solution)/shard_map/bidiagonalise/pallas_call | solution.py:394
  58.8 0.5 slice_bitcast_fusion
  59.3 0.6 copy.9
  59.9 0.6 %copy.10 = f32[16384]{0:T(1024)} copy(f32[16384]{0:T(1024)S(1)} %bitcast.4) | data formatting | bytes 131072
Async XLA Ops:
  0.6 1.0 %copy-start = (f32[4,16384]{1,0:T(4,128)S(1)}, f32[4,16384]{1,0:T(4,128)}, u32[]{:S(2)}) copy-start(f32[4,16384]{1,0:T(4,128)} %mp.1) | copy-start | bytes 786436
  1.6 0.7 %copy-start.1 = (f32[2,256]{1,0:T(2,128)S(1)}, f32[2,256]{1,0:T(2,128)}, u32[]{:S(2)}) copy-start(f32[2,256]{1,0:T(2,128)} %dp_in.1) | copy-start | bytes 6148
  2.3 0.7 %copy-start.2 = (s32[2,32]{1,0:T(2,128)S(1)}, s32[2,32]{1,0:T(2,128)}, u32[]{:S(2)}) copy-start(s32[2,32]{1,0:T(2,128)} %mask_in.1) | copy-start | bytes 772

commit v4 on v3

--- a/solution.py
+++ b/solution.py
@@ -61,13 +61,9 @@
         rows + size == lax.broadcasted_iota(jnp.int32, (size, LANES), 1), 1.0, 0.0
     )
     a = jnp.concatenate([gram, jnp.zeros((size, LANES - size), F32)], axis=1) + unit
-    for i in range(0, size, 2):
-        r0, r1 = a[i : i + 1, :], a[i + 1 : i + 2, :]
-        p, q, r = r0[:, i : i + 1], r0[:, i + 1 : i + 2], r1[:, i + 1 : i + 2]
-        scale = 1.0 / (p * r - q * q)
-        new0, new1 = (r * scale) * r0 - (q * scale) * r1, (p * scale) * r1 - (q * scale) * r0
-        rest = a - a[:, i : i + 1] * new0 - a[:, i + 1 : i + 2] * new1
-        a = jnp.where(rows == i, new0, jnp.where(rows == i + 1, new1, rest))
+    for i in range(size):
+        pivot_row = a[i : i + 1, :] / a[i : i + 1, i : i + 1]
+        a = jnp.where(rows == i, pivot_row, a - a[:, i : i + 1] * pivot_row)
     return jnp.concatenate([a[:, size : 2 * size], jnp.zeros((size, LANES - size), F32)], axis=1)
 
 

time: 60.7 us -> 59.8 us (0.985)
  Pallas kernels: 55.9 us -> 54.9 us
    pallas_call x1, Pallas kernels: 55.9 us -> 54.9 us  [per_device(): pl.pallas_call(functools.partial(kernel, nc, ns, rows * ns, cols * nc), o...]
where the time goes in v4:
time: 59.8 us; the launch traced here: 59.6 us
  Pallas kernels  54.9 us (92%)
  local copies, waits for them, and re-layouts  4.01 us (7%)
  between operations  0.65 us (1%)
    pallas_call x1, Pallas kernels, per_device(): pl.pallas_call(functools.partial(kernel, nc, ns, rows * ns, cols * nc), o...  54.9 us
    unnamed x8, local copies, waits for them, and re-layouts  3.5 us

profile of v4, /device:TPU:1, one launch (start us, length us, event | category | flops | bytes accessed | tf_op | source)
XLA Modules:
  0.0 59.6 jit_solution(3651229288287430176)
XLA Ops:
  0.6 0.0 copy-start
  0.6 0.9 %copy-done = f32[4,16384]{1,0:T(4,128)S(1)} copy-done((f32[4,16384]{1,0:T(4,128)S(1)}, f32[4,16384]{1,0:T(4,128)}, u32[]{:S(2)}) %copy-start) | copy-done | bytes 262168
  1.6 0.0 copy-start.1
  1.6 0.7 %copy-done.1 = f32[2,256]{1,0:T(2,128)S(1)} copy-done((f32[2,256]{1,0:T(2,128)S(1)}, f32[2,256]{1,0:T(2,128)}, u32[]{:S(2)}) %copy-start.1) | copy-done | bytes 2072
  2.3 0.0 copy-start.2
  2.3 0.7 %copy-done.2 = s32[2,32]{1,0:T(2,128)S(1)} copy-done((s32[2,32]{1,0:T(2,128)S(1)}, s32[2,32]{1,0:T(2,128)}, u32[]{:S(2)}) %copy-start.2) | copy-done | bytes 280
  2.9 54.9 %bidiagonalise.1 = (f32[2,128]{1,0:T(2,128)S(1)}, f32[128,128]{1,0:T(8,128)S(1)}, f32[1,128]{1,0:T(1,128)S(1)}) custom-call(f32[256,16384]{1,0:T(8,128)} %sens.1, s32[2,32]{1,0:T(2,128)S(1)} %copy-done.2, f32[2,256]{1,0:T(2,128)S(1)} %copy-done.1, f32[4,16384]{1,0:T(4,128)S(1)} %copy-done), custom_call_target="tpu_custom_call" | custom-call | tf_op jit(solution)/shard_map/bidiagonalise/pallas_call | solution.py:390
  57.9 0.5 slice_bitcast_fusion
  58.4 0.6 copy.9
  59.0 0.6 %copy.10 = f32[16384]{0:T(1024)} copy(f32[16384]{0:T(1024)S(1)} %bitcast.4) | data formatting | bytes 131072
Async XLA Ops:
  0.6 1.0 %copy-start = (f32[4,16384]{1,0:T(4,128)S(1)}, f32[4,16384]{1,0:T(4,128)}, u32[]{:S(2)}) copy-start(f32[4,16384]{1,0:T(4,128)} %mp.1) | copy-start | bytes 786436
  1.6 0.7 %copy-start.1 = (f32[2,256]{1,0:T(2,128)S(1)}, f32[2,256]{1,0:T(2,128)}, u32[]{:S(2)}) copy-start(f32[2,256]{1,0:T(2,128)} %dp_in.1) | copy-start | bytes 6148
  2.3 0.7 %copy-start.2 = (s32[2,32]{1,0:T(2,128)S(1)}, s32[2,32]{1,0:T(2,128)}, u32[]{:S(2)}) copy-start(s32[2,32]{1,0:T(2,128)} %mask_in.1) | copy-start | bytes 772

commit v5 on v4

--- a/solution.py
+++ b/solution.py
@@ -223,9 +223,6 @@
     x_col = t_u[:, size - 1 : size] / jnp.sqrt(t_u[size - 1 : size, size - 1 : size])
     start = [jnp.sum(x_col * p64[h], axis=0, keepdims=True) for h in range(halves)]
 
-    wait_all(5, gmc.at[pl.ds(0, nc - 1)])
-    gms[me_s] = jnp.sum(gmc[...], axis=0)
-    exchange("station", lambda peer: gms.at[me_s], gms.at[me_s], 6)
     load_mask.wait()
     for copy in loads:
         copy.wait()
@@ -333,6 +330,9 @@
         return rest, mine_u, norm_u, norm_v, scale
 
     adjoint(start, 0, 7)
+    wait_all(5, gmc.at[pl.ds(0, nc - 1)])
+    gms[me_s] = jnp.sum(gmc[...], axis=0)
+    exchange("station", lambda peer: gms.at[me_s], gms.at[me_s], 6)
     bulk_relay()
     w_own = gather(0, 7, 8)
     share_coef(0, panel_coef(pown, w_own), 9)

time: 59.8 us -> 59.8 us (level)
  no operation moved by 1% of the time
where the time goes in v5:
time: 59.8 us; the launch traced here: 59.6 us
  Pallas kernels  55 us (92%)
  local copies, waits for them, and re-layouts  4.01 us (7%)
  between operations  0.65 us (1%)
    pallas_call x1, Pallas kernels, per_device(): pl.pallas_call(functools.partial(kernel, nc, ns, rows * ns, cols * nc), o...  55 us
    unnamed x8, local copies, waits for them, and re-layouts  3.5 us

profile of v5, /device:TPU:1, one launch (start us, length us, event | category | flops | bytes accessed | tf_op | source)
XLA Modules:
  0.0 59.6 jit_solution(4620671959182234210)
XLA Ops:
  0.6 0.0 copy-start
  0.6 0.9 %copy-done = f32[4,16384]{1,0:T(4,128)S(1)} copy-done((f32[4,16384]{1,0:T(4,128)S(1)}, f32[4,16384]{1,0:T(4,128)}, u32[]{:S(2)}) %copy-start) | copy-done | bytes 262168
  1.6 0.0 copy-start.1
  1.6 0.7 %copy-done.1 = f32[2,256]{1,0:T(2,128)S(1)} copy-done((f32[2,256]{1,0:T(2,128)S(1)}, f32[2,256]{1,0:T(2,128)}, u32[]{:S(2)}) %copy-start.1) | copy-done | bytes 2072
  2.3 0.0 copy-start.2
  2.3 0.7 %copy-done.2 = s32[2,32]{1,0:T(2,128)S(1)} copy-done((s32[2,32]{1,0:T(2,128)S(1)}, s32[2,32]{1,0:T(2,128)}, u32[]{:S(2)}) %copy-start.2) | copy-done | bytes 280
  2.9 55.0 %bidiagonalise.1 = (f32[2,128]{1,0:T(2,128)S(1)}, f32[128,128]{1,0:T(8,128)S(1)}, f32[1,128]{1,0:T(1,128)S(1)}) custom-call(f32[256,16384]{1,0:T(8,128)} %sens.1, s32[2,32]{1,0:T(2,128)S(1)} %copy-done.2, f32[2,256]{1,0:T(2,128)S(1)} %copy-done.1, f32[4,16384]{1,0:T(4,128)S(1)} %copy-done), custom_call_target="tpu_custom_call" | custom-call | tf_op jit(solution)/shard_map/bidiagonalise/pallas_call | solution.py:390
  57.9 0.5 slice_bitcast_fusion
  58.4 0.6 copy.9
  59.0 0.6 %copy.10 = f32[16384]{0:T(1024)} copy(f32[16384]{0:T(1024)S(1)} %bitcast.4) | data formatting | bytes 131072
Async XLA Ops:
  0.6 1.0 %copy-start = (f32[4,16384]{1,0:T(4,128)S(1)}, f32[4,16384]{1,0:T(4,128)}, u32[]{:S(2)}) copy-start(f32[4,16384]{1,0:T(4,128)} %mp.1) | copy-start | bytes 786436
  1.6 0.7 %copy-start.1 = (f32[2,256]{1,0:T(2,128)S(1)}, f32[2,256]{1,0:T(2,128)}, u32[]{:S(2)}) copy-start(f32[2,256]{1,0:T(2,128)} %dp_in.1) | copy-start | bytes 6148
  2.3 0.7 %copy-start.2 = (s32[2,32]{1,0:T(2,128)S(1)}, s32[2,32]{1,0:T(2,128)}, u32[]{:S(2)}) copy-start(s32[2,32]{1,0:T(2,128)} %mask_in.1) | copy-start | bytes 772
